TPU v7x, 256 devices: a whole 4x4x8 slice. The times are simulated.
256 devices in a mesh: tm: 4 (over y_lo, core), pts: 64 (over y_hi, z, x).
Axes of the slice: x: 4, y: 4 (y_hi: 2, y_lo: 2; y = y_hi * 2 + y_lo), z: 8, core: 2. Of those that a mesh axis runs over, the one named last changes fastest.
Arguments:
- saved_paths: bfloat16 [4096, 64, 512], P('tm', 'pts')
- pca_basis: bfloat16 [4096, 4096], P('pts', 'tm')
- vol_surface: float32 [4096, 512], P('tm'), may hold values from 0.5 to 2
- chol_factor: bfloat16 [512, 512], replicated
- exposure_load: float32 [32, 512], replicated, may hold values from -0.25 to 0.25
- reset_load: float32 [32, 512], replicated, may hold values from -0.0234375 to 0.0234375
- strikes: float32 [32], replicated, may hold values from -4 to 4
- bucket_weight: float32 [32], replicated, may hold values from 0.5 to 2
- bucket_start: int32 [32], replicated, may hold values from 0 to 4095, as said below
- generator: int32 [512], replicated, may hold values from 1 to 1048575
- point_ids: int32 [64], P('pts'), may hold values from 0 to 1048575
Outputs:
- normal_adjoint: float32 [4096, 64, 512], P('tm', 'pts')
- vol_greeks: float32 [4096, 512], P('tm')
- chol_greeks: float32 [512, 512], replicated
Inputs may be any that keep to these rules, and one draw needn't show every extreme that they name: bucket_start[0] = 0, the last entry is 4095, and the entries rise strictly.
All inputs are finite; a program needn't handle non-finite values.
Results may differ from a plain program's by a relative error of at most 0.0042.
Values may be sent and summed in bfloat16 or wider, within the bound.
No kernel may reach another device: no remote copies, remote signals or barrier semaphores. Data moves between devices by JAX's collectives and lax.ppermute only.
A program may use at most 128 MiB of HBM per device.

v0:
```python
import jax
import jax.numpy as jnp
from jax import lax
from jax.sharding import PartitionSpec as P


def lattice_shift(point_ids, generator):
    gen_low = generator % 1024
    gen_high = generator // 1024
    low_part = point_ids[:, None] * gen_low[None, :] % 1048576
    high_part = point_ids[:, None] * gen_high[None, :] % 1024 * 1024
    residue = (low_part + high_part) % 1048576
    uniform_pts = (residue.astype(jnp.float32) + 0.5) / 1048576.0
    return 0.5 * 3.4641016151377544 * (uniform_pts - 0.5)


def body(
    saved_paths,
    pca_basis,
    vol_surface,
    chol_factor,
    exposure_load,
    reset_load,
    strikes,
    bucket_weight,
    bucket_start,
    generator,
    point_ids,
):
    highest = lax.Precision.HIGHEST
    steps_loc, point_count, factor_count = saved_paths.shape
    total_steps = steps_loc * lax.axis_size("tm")
    basis_full = lax.all_gather(pca_basis, "pts", axis=0, tiled=True)
    own_basis = lax.all_to_all(basis_full, "tm", split_axis=0, concat_axis=1, tiled=True)
    step_index = lax.axis_index("tm") * steps_loc + jnp.arange(steps_loc, dtype=jnp.int32)
    next_start = jnp.concatenate([bucket_start[1:], jnp.full((1,), total_steps, jnp.int32)])
    member = (
        (step_index[:, None] >= bucket_start[None, :]) & (step_index[:, None] < next_start[None, :])
    ).astype(jnp.float32)
    at_start = (step_index[:, None] == bucket_start[None, :]).astype(jnp.float32)
    start_state = lattice_shift(point_ids, generator)
    flat_paths = saved_paths.reshape(steps_loc * point_count, factor_count)
    factor_level = jnp.dot(flat_paths, chol_factor.T, preferred_element_type=jnp.float32).reshape(
        steps_loc, point_count, factor_count
    )
    path_state = start_state[None, :, :] + vol_surface[:, None, :] * factor_level
    local_reset = jnp.einsum("te,tpf->epf", at_start, path_state, precision=highest)
    reset_state = lax.psum(local_reset, "tm")
    load_steps = jnp.dot(member, exposure_load, precision=highest)
    reset_term = jnp.sum(reset_load[:, None, :] * reset_state, axis=2)
    margin = (
        jnp.sum(load_steps[:, None, :] * path_state, axis=2)
        + jnp.dot(member, reset_term, precision=highest)
        - jnp.dot(member, strikes, precision=highest)[:, None]
    )
    sensitivity = jnp.dot(member, bucket_weight, precision=highest)[:, None] * jax.nn.sigmoid(
        margin
    )
    bucket_sens = lax.psum(jnp.dot(member.T, sensitivity, precision=highest), "tm")
    reset_adj = bucket_sens[:, :, None] * reset_load[:, None, :]
    adj_state = sensitivity[:, :, None] * load_steps[:, None, :] + jnp.einsum(
        "te,epf->tpf", at_start, reset_adj, precision=highest
    )
    vol_local = jnp.sum(adj_state * factor_level, axis=1)
    scaled_adj = (vol_surface[:, None, :] * adj_state).astype(jnp.bfloat16)
    flat_scaled = scaled_adj.reshape(steps_loc * point_count, factor_count)
    chol_local = jnp.dot(flat_scaled.T, flat_paths, preferred_element_type=jnp.float32)
    adj_path = jnp.dot(flat_scaled, chol_factor, preferred_element_type=jnp.float32).astype(
        jnp.bfloat16
    )
    empty_adj = jnp.zeros((steps_loc, point_count, factor_count), jnp.float32)
    adj_rows = adj_path.reshape(steps_loc, point_count, factor_count)
    block_in = lax.all_gather(adj_rows, "tm", axis=0, tiled=True)
    block_rows = block_in.shape[0]
    product = jnp.dot(
        own_basis,
        block_in.reshape(block_rows, point_count * factor_count),
        preferred_element_type=jnp.float32,
    )
    normal_adjoint = product.reshape(empty_adj.shape)
    vol_greeks = lax.psum(vol_local, "pts")
    chol_total = lax.psum(chol_local, ("tm", "pts"))
    chol_greeks = chol_total / total_steps
    return (normal_adjoint, vol_greeks, chol_greeks)


def solution(mesh):
    return jax.shard_map(
        body,
        mesh=mesh,
        in_specs=(
            P("tm", "pts", None),
            P("pts", "tm"),
            P("tm", None),
            P(),
            P(),
            P(),
            P(),
            P(),
            P(),
            P(),
            P("pts"),
        ),
        out_specs=(P("tm", "pts", None), P("tm", None), P()),
        check_vma=False,
    )
```

profile of v0, /device:TPU:2, one launch (start us, length us, event | category | flops | bytes accessed | tf_op | source)
XLA Modules:
  0.0 1129.2 jit_solution(17987239232640617010)
XLA Ops:
  8.0 0.0 copy-start
  8.0 0.0 all-reduce.4.cloned.1.call-start
  8.8 0.0 copy-start.8
  8.8 2.9 copy.26
  11.7 0.0 copy-start.1
  11.7 0.0 copy-start.7
  11.7 0.0 copy-done.8
  11.7 0.0 copy-done
  11.7 1.9 fusion.2
  13.7 0.0 copy-done.1
  13.7 0.0 copy-done.7
  13.7 0.0 copy-start.9
  13.7 0.0 copy-start.10
  13.7 0.0 copy-start.6
  13.7 2.1 convolution_bitcast_fusion.1
  15.8 0.0 all-reduce.4.cloned.1.call-update
  15.9 0.0 all-gather.4.cloned.1.call-start
  15.9 0.5 all-gather.4.cloned.1.call-update
  16.4 0.0 all-reduce.8.cloned.1.call-start
  16.5 0.1 slice.3
  16.6 0.1 pad_add_fusion
  16.6 0.0 copy-done.9
  16.6 0.4 fusion.26
  17.1 0.0 copy-done.10
  17.1 0.5 fusion.30
  17.6 0.0 copy-done.6
  17.6 0.0 copy-start.5
  17.6 4.3 multiply_reduce_fusion
  21.9 37.8 %all-reduce.4.cloned.1.call-done = f32[32,1,512]{2,0,1:T(8,128)} async-done(((f32[32,1,512]{2,0,1:T(8,128)}), f32[32,1,512]{2,0,1:T(8,128)}) %all-reduce.4.cloned.1.call-update) | async-done | bytes 65552 | tf_op jit(solution)/shard_map/psum | solution.py:48
  59.6 0.0 copy-done.5
  59.6 1.0 fusion.9
  60.6 0.5 fusion.28
  61.1 0.4 convolution_bitcast_fusion.2
  61.5 6.3 psum.29
  67.8 5.0 fusion.33
  72.8 0.0 copy-start.2
  72.8 1.0 copy-done.2
  73.7 1.7 fusion
  75.5 0.0 all-reduce.8.cloned.1.call-update
  75.5 0.0 all-reduce.6.cloned.1.call-start
  75.5 0.7 all-reduce.6.cloned.1.call-update
  76.2 94.7 %all-gather.4.cloned.1.call-done = bf16[4096,1024]{1,0:T(8,128)(2,1)} async-done(((bf16[64,1024]{1,0:T(8,128)(2,1)}), bf16[4096,1024]{1,0:T(8,128)(2,1)}) %all-gather.4.cloned.1.call-update) | async-done | bytes 8388624 | tf_op jit(solution)/shard_map/all_gather | solution.py:33
  171.0 0.0 copy-start.3
  171.0 0.0 copy-start.4
  171.0 5.8 all-to-all-start
  176.8 0.0 all-gather.6.cloned.1.call-start
  176.8 0.0 copy-done.3
  176.8 0.0 copy-done.4
  176.9 1.7 convolution_convert_fusion
  178.6 0.0 all-gather.6.cloned.1.call-update
  178.6 183.0 %all-reduce.8.cloned.1.call-done = f32[512,512]{1,0:T(8,128)} async-done(((f32[512,512]{1,0:T(8,128)}), f32[512,512]{1,0:T(8,128)}) %all-reduce.8.cloned.1.call-update) | async-done | bytes 1048592 | tf_op jit(solution)/shard_map/psum | solution.py:82
  361.6 2.3 broadcast_multiply_fusion
  363.9 696.8 %all-reduce.6.cloned.1.call-done = f32[1024,512]{0,1:T(8,128)} async-done(((f32[1024,512]{0,1:T(8,128)}), f32[1024,512]{0,1:T(8,128)}) %all-reduce.6.cloned.1.call-update) | async-done | bytes 2097168 | tf_op jit(solution)/shard_map/psum | solution.py:81
  1060.7 2.9 copy.29
  1063.6 0.0 all-to-all-done
  1063.6 11.5 %copy.27 = bf16[1024,4,1024]{0,2,1:T(8,128)(2,1)} copy(bf16[1024,4,1024]{2,0,1:T(8,128)(2,1)} %bitcast.13) | data formatting | bytes 16777216 | tf_op jit(solution)/shard_map/all_to_all | solution.py:34
  1075.1 35.1 %all-gather.6.cloned.1.call-done = bf16[4096,512]{1,0:T(8,128)(2,1)} async-done(((bf16[1024,512]{1,0:T(8,128)(2,1)}), bf16[4096,512]{1,0:T(8,128)(2,1)}) %all-gather.6.cloned.1.call-update) | async-done | bytes 4194320 | tf_op jit(solution)/shard_map/all_gather | solution.py:73
  1110.2 8.2 convolution_bitcast_fusion
  1118.4 3.7 copy.28
  (3 shorter events, 0.1 us)
Async XLA Ops:
  8.0 3.7 copy-start
  8.0 51.6 %all-reduce.4.cloned.1.call-start = ((), (), s32[]{:S(2)}) async-start(), calls=%async_computation.1 | async-start | bytes 131072 | tf_op jit(solution)/shard_map/psum | solution.py:48
  8.8 2.9 copy-start.8
  11.7 2.0 copy-start.1
  11.7 2.0 copy-start.7
  13.7 2.9 copy-start.9
  13.7 3.4 copy-start.10
  13.7 3.8 copy-start.6
  15.9 155.1 %all-gather.4.cloned.1.call-start = ((), (), s32[]{:S(2)}) async-start(), calls=%async_computation.2 | async-start | bytes 8519680 | tf_op jit(solution)/shard_map/all_gather | solution.py:33
  16.4 345.2 %all-reduce.8.cloned.1.call-start = ((), (), s32[]{:S(2)}) async-start(), calls=%async_computation.4 | async-start | bytes 2097152 | tf_op jit(solution)/shard_map/psum | solution.py:82
  17.6 42.1 %copy-start.5 = (f32[32,512]{1,0:T(8,128)S(1)}, f32[32,512]{1,0:T(8,128)}, u32[]{:S(2)}) copy-start(f32[32,512]{1,0:T(8,128)} %param.16) | copy-start | bytes 196612
  72.8 1.0 copy-start.2
  75.5 985.2 %all-reduce.6.cloned.1.call-start = ((), (), s32[]{:S(2)}) async-start(), calls=%async_computation.3 | async-start | bytes 4194304 | tf_op jit(solution)/shard_map/psum | solution.py:81
  171.0 5.9 copy-start.3
  171.0 5.9 copy-start.4
  171.0 892.6 %all-to-all-start = ((bf16[4,1024,1024]{2,1,0:T(8,128)(2,1)}), bf16[4,1024,1024]{2,1,0:T(8,128)(2,1)}, u32[]{:S(2)}, u32[]{:S(2)}) async-start(bf16[4,1024,1024]{2,1,0:T(8,128)(2,1)} %bitcast.43), calls=%async_computation | async-start | bytes 16777216 | tf_op jit(solution)/shard_map/all_to_all | solution.py:34
  176.8 933.4 %all-gather.6.cloned.1.call-start = ((), (), s32[]{:S(2)}) async-start(), calls=%async_computation.5 | async-start | bytes 5242880 | tf_op jit(solution)/shard_map/all_gather | solution.py:73
Sparse Core Ops, SparseCore 0:
  16.0 43.6 all-reduce.3
  75.6 285.9 all-reduce.7
  364.8 695.8 all-reduce.5
  1063.1 47.0 all-gather.5
Sparse Core Ops, SparseCore 1:
  20.4 150.5 all-gather.3
where the time goes:
time: 1130 us
  waiting for transfers between devices  1050 us (93%)
  matrix products  26.7 us (2%)
  local copies, waits for them, and re-layouts  22 us (2%)
  between operations  16.1 us (1%)
    psum x1, waiting for transfers between devices, body(): vol_greeks = lax.psum(vol_local, 'pts')  697 us
    psum x1, waiting for transfers between devices, body(): chol_total = lax.psum(chol_local, ('tm', 'pts'))  183 us
    all_gather x1, waiting for transfers between devices, body(): basis_full = lax.all_gather(pca_basis, 'pts', axis=0, tiled=True)  94.7 us
    psum x1, waiting for transfers between devices, body(): reset_state = lax.psum(local_reset, 'tm')  37.8 us
    all_gather x1, waiting for transfers between devices, body(): block_in = lax.all_gather(adj_rows, 'tm', axis=0, tiled=True)  35.1 us
  transfers between devices with their start and end apart: 6, of which 5 were waited for; matrix products, arithmetic and copies ran while one was open for 3% of the time, Pallas kernels for 0%

commit v1 on v0

v1 whole, which is shorter than its diff:
```python
import jax
import jax.numpy as jnp
from jax import lax
from jax.experimental import pallas as pl
from jax.experimental.pallas import tpu as pltpu
from jax.sharding import Mesh, PartitionSpec as P

BF = jnp.bfloat16
F32 = jnp.float32
ALL = ("yl", "c", "yh", "z", "x")
TM = ("yl", "c")
PTS = ("yh", "z", "x")
BUCKETS = 32
STEPS = 1024
BLOCKS = 4
CHUNK = 256
CHUNKS = STEPS // CHUNK
NF = 512
WROWS = 5 * BUCKETS
VMEM_LIMIT = 48 * 1024 * 1024

NN = (((1,), (0,)), ((), ()))
NT = (((1,), (1,)), ((), ()))
TN = (((0,), (0,)), ((), ()))


def dot(a, b, dims):
    return lax.dot_general(a, b, dims, preferred_element_type=F32)


def split2(x):
    hi = x.astype(BF)
    return hi, (x - hi.astype(F32)).astype(BF)


def one_hots(first_step, count, start, nxt):
    t = first_step + lax.broadcasted_iota(jnp.int32, (BUCKETS, count), 1)
    member = jnp.where((t >= start) & (t < nxt), 1.0, 0.0)
    at_start = jnp.where(t == start, 1.0, 0.0)
    return member, at_start


def margin_kernel(pos, paths, vol, chol, start_state, load, reset, bstart, bnext, out):
    i = pl.program_id(0)
    level = dot(paths[...], chol[...], NT)
    state = start_state[...] + vol[...] * level
    s1, s2 = split2(state)
    l1, l2 = split2(load[...])
    r1, r2 = split2(reset[...])
    big = dot(jnp.concatenate([l1, l2, r1, r2], axis=0), s1, NT)
    small = dot(jnp.concatenate([l1, r1], axis=0), s2, NT)
    n = BUCKETS
    m = big[0:n] + big[n : 2 * n] + small[0:n]
    r = big[2 * n : 3 * n] + big[3 * n : 4 * n] + small[n : 2 * n]
    member, at_start = one_hots(pos[0] * STEPS + i * CHUNK, CHUNK, bstart[...], bnext[...])
    out[0:1, :] = jnp.sum(member * m, axis=0, keepdims=True)
    out[1:2, :] = jnp.sum(at_start * r, axis=0, keepdims=True)


def sens_kernel(
    pos, y, paths, vol, chol, load, reset, strikes, weight, bstart, bnext, wt, bmat, vl, cg, acc
):
    i = pl.program_id(0)

    @pl.when(i == 0)
    def _():
        hots = [one_hots(b * STEPS, STEPS, bstart[...], bnext[...]) for b in range(BLOCKS)]
        l1, l2 = split2(load[...])
        for q in range(2):
            term = sum(
                jnp.sum(hots[b][1] * y[b, q, 1:2, :], axis=1, keepdims=True) for b in range(BLOCKS)
            )
            offset = term - strikes[...]
            total = jnp.zeros((BUCKETS, 1), F32)
            for b in range(BLOCKS):
                member, at_start = hots[b]
                margin = y[b, q, 0:1, :] + jnp.sum(member * offset, axis=0, keepdims=True)
                gain = jnp.sum(member * weight[...], axis=0, keepdims=True)
                ms = member * (gain * jax.nn.sigmoid(margin))
                total = total + jnp.sum(ms, axis=1, keepdims=True)
                m1, m2 = split2(ms)
                a = at_start.astype(BF)
                wt[q, b] = jnp.concatenate([m1, m1, m2, a, a], axis=0)
            r1, r2 = split2(total * reset[...])
            bmat[q] = jnp.concatenate([l1, l2, l1, r1, r2], axis=0)
        acc[...] = jnp.zeros_like(acc)

    lanes = pl.ds(pl.multiple_of(i * CHUNK, CHUNK), CHUNK)
    adj = dot(wt[pos[1], pos[0], :, lanes], bmat[pos[1]], TN)
    level = dot(paths[...], chol[...], NT)
    vl[...] = (adj * level).astype(BF)
    scaled = (vol[...] * adj).astype(BF)
    acc[...] += dot(scaled, paths[...], TN)

    @pl.when(i == CHUNKS - 1)
    def _():
        cg[...] = acc[...].astype(BF)


def adjoint_kernel(pos, basis, v0, v1, v2, v3, wt, bmat, chol, own, other, acc):
    r = pl.program_id(0)
    b = jnp.where(r == 0, pos[2], jnp.where(r == 1, pos[3], jnp.where(r == 2, pos[4], pos[5])))

    @pl.when(r == 0)
    def _():
        acc[...] = jnp.zeros_like(acc)

    for k, v in enumerate((v0, v1, v2, v3)):

        @pl.when(r == k)
        def _(v=v):
            for j in range(CHUNKS):
                rows = pl.ds(j * CHUNK, CHUNK)
                vol = v[rows, :].astype(F32)
                for q in range(2):
                    adj = dot(wt[q, b, :, rows], bmat[q], TN)
                    scaled = (vol * adj).astype(BF)
                    acc[q] += dot(basis[0, :, rows], scaled, NN)

    @pl.when(r == BLOCKS - 1)
    def _():
        for q in range(2):
            h1, h2 = split2(acc[q])
            res = dot(h1, chol[...], NN) + dot(h2, chol[...], NN)

            @pl.when(pos[1] == q)
            def _():
                own[...] = res

            @pl.when(pos[1] != q)
            def _():
                other[...] = res.astype(BF)


def full(shape):
    return pl.BlockSpec(shape, lambda *_: (0,) * len(shape))


SMEM = pl.BlockSpec(memory_space=pltpu.SMEM)
PARAMS = pltpu.CompilerParams(vmem_limit_bytes=VMEM_LIMIT)


def lattice_shift(point_ids, generator):
    gen_low = generator % 1024
    gen_high = generator // 1024
    low_part = point_ids[:, None] * gen_low[None, :] % 1048576
    high_part = point_ids[:, None] * gen_high[None, :] % 1024 * 1024
    residue = (low_part + high_part) % 1048576
    uniform_pts = (residue.astype(F32) + 0.5) / 1048576.0
    return 0.5 * 3.4641016151377544 * (uniform_pts - 0.5)


def flip(axis):
    return [(0, 1), (1, 0)]


def basis_moves():
    moves = []
    for yl in range(2):
        for c in range(2):
            for yh in range(2):
                for z in range(8):
                    for x in range(4):
                        src = (((yl * 2 + c) * 2 + yh) * 8 + z) * 4 + x
                        z2, z1, z0 = z >> 2, (z >> 1) & 1, z & 1
                        to_yl, to_c, to_yh = yh, z2, z1
                        to_z = ((yl ^ to_yl) * 2 + (c ^ to_c)) * 2 + z0
                        moves.append((src, (((to_yl * 2 + to_c) * 2 + to_yh) * 8 + to_z) * 4 + x))
    return moves


def exchange(parts, axis, size):
    return lax.all_to_all(parts, axis, split_axis=0, concat_axis=0, tiled=True)


def gather(x, axis, size):
    return lax.all_to_all(
        jnp.broadcast_to(x[None], (size,) + x.shape), axis, split_axis=0, concat_axis=0, tiled=True
    )


def body(
    saved_paths,
    pca_basis,
    vol_surface,
    chol_factor,
    exposure_load,
    reset_load,
    strikes,
    bucket_weight,
    bucket_start,
    generator,
    point_ids,
):
    yl, c, yh = lax.axis_index("yl"), lax.axis_index("c"), lax.axis_index("yh")
    block = yl * 2 + c
    pos = jnp.stack([block, yh, block, block ^ 1, block ^ 2, block ^ 3]).astype(jnp.int32)
    paths = saved_paths.reshape(STEPS, NF)
    bstart = bucket_start[:, None]
    bnext = jnp.concatenate([bucket_start[1:], jnp.full((1,), BLOCKS * STEPS, jnp.int32)])[:, None]
    start_state = lattice_shift(point_ids, generator)

    moved = lax.ppermute(pca_basis, ALL, basis_moves())
    basis = lax.all_gather(moved, ("z", "x"), axis=0, tiled=True).reshape(BLOCKS, STEPS // 2, STEPS)

    v0 = vol_surface.astype(BF)
    v2 = lax.ppermute(v0, "yl", flip("yl"))
    v1 = lax.ppermute(v0, "c", flip("c"))
    v3 = lax.ppermute(v2, "c", flip("c"))

    rows = pl.BlockSpec((CHUNK, NF), lambda i: (i, 0))
    bucket_rows = full((BUCKETS, NF))
    bucket_col = full((BUCKETS, 1))
    square = full((NF, NF))
    y_own = pl.pallas_call(
        margin_kernel,
        grid=(CHUNKS,),
        in_specs=[SMEM, rows, rows, square, full((1, NF)), bucket_rows, bucket_rows, bucket_col, bucket_col],
        out_specs=pl.BlockSpec((2, CHUNK), lambda i: (0, i)),
        out_shape=jax.ShapeDtypeStruct((2, STEPS), F32),
        compiler_params=PARAMS,
        name="margins",
    )(pos, paths, vol_surface, chol_factor, start_state, exposure_load, reset_load, bstart, bnext)
    y_all = lax.all_gather(y_own, ("yl", "c", "yh"), axis=0).reshape(BLOCKS, 2, 2, STEPS)

    wt, bmat, vol_part, chol_part = pl.pallas_call(
        sens_kernel,
        grid=(CHUNKS,),
        in_specs=[SMEM, full((BLOCKS, 2, 2, STEPS)), rows, rows, square, bucket_rows, bucket_rows]
        + [bucket_col] * 4,
        out_specs=[full((2, BLOCKS, WROWS, STEPS)), full((2, WROWS, NF)), rows, square],
        out_shape=[
            jax.ShapeDtypeStruct((2, BLOCKS, WROWS, STEPS), BF),
            jax.ShapeDtypeStruct((2, WROWS, NF), BF),
            jax.ShapeDtypeStruct((STEPS, NF), BF),
            jax.ShapeDtypeStruct((NF, NF), BF),
        ],
        scratch_shapes=[pltpu.VMEM((NF, NF), F32)],
        compiler_params=PARAMS,
        name="sensitivities",
    )(
        pos, y_all, paths, vol_surface, chol_factor, exposure_load, reset_load,
        strikes[:, None], bucket_weight[:, None], bstart, bnext,
    )

    half = NF // 2
    kept = lax.dynamic_slice_in_dim(chol_part, c * half, half, 0).astype(F32)
    sent = lax.dynamic_slice_in_dim(chol_part, (1 - c) * half, half, 0)
    chol_half = (kept + lax.ppermute(sent, "c", flip("c")).astype(F32)).astype(BF)
    parts = jnp.concatenate([vol_part.reshape(4, 256, NF), chol_half.reshape(4, 64, NF)], axis=1)
    over_x = jnp.sum(exchange(parts, "x", 4).astype(F32), axis=0).astype(BF)
    parts = jnp.concatenate(
        [over_x[:256].reshape(8, 32, NF), over_x[256:].reshape(8, 8, NF)], axis=1
    )
    over_z = jnp.sum(exchange(parts, "z", 8).astype(F32), axis=0)
    parts = jnp.concatenate([over_z[:32].reshape(2, 16, NF), over_z[32:].reshape(2, 4, NF)], axis=1)
    kept = lax.dynamic_index_in_dim(parts, yh, 0, keepdims=False)
    sent = lax.dynamic_index_in_dim(parts, 1 - yh, 0, keepdims=False)
    mine = kept + lax.ppermute(sent, "yh", flip("yh"))
    chol_rows = mine[16:] + lax.ppermute(mine[16:], "yl", flip("yl"))
    mine = jnp.concatenate([mine[:16], chol_rows], axis=0).astype(BF)
    theirs = lax.ppermute(mine, "yh", flip("yh"))
    pair = jnp.where(yh == 0, jnp.stack([mine, theirs]), jnp.stack([theirs, mine]))
    all_z = gather(pair, "z", 8)
    all_x = gather(all_z, "x", 4)
    vol_greeks = all_x[:, :, :, :16].reshape(STEPS, NF).astype(F32)
    chol_mine = all_x[:, :, :, 16:].reshape(half, NF)
    chol_theirs = lax.ppermute(chol_mine, "c", flip("c"))
    chol_greeks = (
        jnp.where(
            c == 0,
            jnp.concatenate([chol_mine, chol_theirs]),
            jnp.concatenate([chol_theirs, chol_mine]),
        ).astype(F32)
        / (BLOCKS * STEPS)
    )

    own, other = pl.pallas_call(
        adjoint_kernel,
        grid=(BLOCKS,),
        in_specs=[SMEM, pl.BlockSpec((1, STEPS // 2, STEPS), lambda i: (i, 0, 0))]
        + [full((STEPS, NF))] * 4
        + [full((2, BLOCKS, WROWS, STEPS)), full((2, WROWS, NF)), square],
        out_specs=[full((STEPS // 2, NF))] * 2,
        out_shape=[
            jax.ShapeDtypeStruct((STEPS // 2, NF), F32),
            jax.ShapeDtypeStruct((STEPS // 2, NF), BF),
        ],
        scratch_shapes=[pltpu.VMEM((2, STEPS // 2, NF), F32)],
        compiler_params=PARAMS,
        name="adjoints",
    )(pos, basis, v0, v1, v2, v3, wt, bmat, chol_factor)
    got = lax.ppermute(other, "yh", flip("yh")).astype(F32)
    normal_adjoint = jnp.where(yh == 0, jnp.stack([own, got]), jnp.stack([got, own]))
    return normal_adjoint.reshape(STEPS, 1, NF), vol_greeks, chol_greeks


def solution(mesh):
    split = Mesh(mesh.devices.reshape(2, 2, 2, 8, 4), ALL)
    return jax.shard_map(
        body,
        mesh=split,
        in_specs=(
            P(TM, PTS, None),
            P(PTS, TM),
            P(TM, None),
            P(),
            P(),
            P(),
            P(),
            P(),
            P(),
            P(),
            P(PTS),
        ),
        out_specs=(P(TM, PTS, None), P(TM, None), P()),
        check_vma=False,
    )
```

time: 1130 us -> 219 us (0.19)
  waiting for transfers between devices: 1050 us -> 48.6 us
  blocking collectives: 6.31 us -> 74 us
  matrix products: 26.7 us -> 0 us
  Pallas kernels: 0 us -> 24.5 us
  starting transfers between devices: 6.02 us -> 30.3 us
    psum x3 -> x0, waiting for transfers between devices: 918 us -> none  [the longest x1 697 us: body(): vol_greeks = lax.psum(vol_local, 'pts')]
    all_gather x2 -> x1, waiting for transfers between devices: 130 us -> 0.02 us  [body(): lax.all_gather(moved, ('z', 'x'), axis=0, tiled=True)]
    all_gather x0 -> x1, blocking collectives: none -> 38.6 us  [body(): lax.all_gather(y_own, ('yl', 'c', 'yh'), axis=0)]
    all_to_all x0 -> x1, blocking collectives: none -> 35.4 us  [exchange(): return lax.all_to_all(parts, axis, split_axis=0, concat_axis=0, tiled=True)]
    dot_general x11 -> x0, matrix products: 26.7 us -> none  [the longest x1 8.21 us: body(): jnp.dot(own_basis, block_in.reshape(block_rows, point_count * factor_coun...]
    ppermute x0 -> x10, waiting for transfers between devices: none -> 25.2 us  [the longest x1 16.5 us: body(): theirs = lax.ppermute(mine, 'yh', flip('yh'))]
    pallas_call x0 -> x3, Pallas kernels: none -> 24.5 us  [the longest x1 16.1 us: body(): pl.pallas_call(adjoint_kernel, grid=(BLOCKS,), in_specs=[SMEM, pl.BlockSp...]
    all_to_all x1 -> x3, waiting for transfers between devices: 0.01 us -> 23.4 us  [the longest x1 12.7 us: exchange(): return lax.all_to_all(parts, axis, split_axis=0, concat_axis=0, tiled=True)]
  transfers between devices with their start and end apart: 6 -> 14, of which waited for: 5 -> 7; matrix products, arithmetic and copies ran while one was open for 3% -> 7% of each run, Pallas kernels for 0% -> 11%
where the time goes in v1:
time: 219 us; the launch traced here: 218 us
  blocking collectives  74 us (34%)
  waiting for transfers between devices  48.6 us (22%)
  starting transfers between devices  30.3 us (14%)
  Pallas kernels  24.5 us (11%)
  local copies, waits for them, and re-layouts  18.8 us (9%)
  between operations  14.9 us (7%)
  other arithmetic  6.91 us (3%)
    all_gather x1, blocking collectives, body(): lax.all_gather(y_own, ('yl', 'c', 'yh'), axis=0)  38.6 us
    all_to_all x1, blocking collectives, exchange(): return lax.all_to_all(parts, axis, split_axis=0, concat_axis=0, tiled=True)  35.4 us
    ppermute x1, waiting for transfers between devices, body(): theirs = lax.ppermute(mine, 'yh', flip('yh'))  16.5 us
    pallas_call x1, Pallas kernels, body(): pl.pallas_call(adjoint_kernel, grid=(BLOCKS,), in_specs=[SMEM, pl.BlockSp...  16.1 us
    all_to_all x1, waiting for transfers between devices, exchange(): return lax.all_to_all(parts, axis, split_axis=0, concat_axis=0, tiled=True)  12.7 us
    unnamed x26, local copies, waits for them, and re-layouts  11 us
    all_to_all x2, waiting for transfers between devices, gather(): lax.all_to_all(jnp.broadcast_to(x[None], (size,) + x.shape), axis, split_...  10.7 us
    all_to_all x2, starting transfers between devices, gather(): lax.all_to_all(jnp.broadcast_to(x[None], (size,) + x.shape), axis, split_...  9.42 us
  transfers between devices with their start and end apart: 14, of which 7 were waited for; matrix products, arithmetic and copies ran while one was open for 7% of the time, Pallas kernels for 11%

profile of v1, /device:TPU:2, one launch (start us, length us, event | category | flops | bytes accessed | tf_op | source)
XLA Modules:
  0.0 218.0 jit_solution(13924795840528629809)
XLA Ops:
  7.2 0.0 all-gather.4.cloned.1.call-start
  7.2 1.6 collective-permute-start
  8.8 0.0 collective-permute-done
  8.8 0.6 copy-done.11
  9.4 0.0 all-gather.4.cloned.1.call-update
  10.1 0.7 slice.28
  10.8 0.7 copy.42.bstart
  11.6 0.1 add_bitcast_fusion
  11.7 0.1 copy.43.bnext
  11.7 0.7 copy.44.strikes
  12.5 0.7 copy.45.weight
  13.2 0.1 stack.53.pos
  13.3 0.7 fusion.16
  14.0 1.6 copy-done
  15.6 1.0 copy-done.2
  16.6 1.2 copy-done.4
  17.9 0.8 copy-done.7
  18.7 0.8 copy-done.9
  19.6 3.1 %margins.1 = f32[2,1024]{1,0:T(2,128)S(1)} custom-call(s32[6]{0:T(128)S(1)} %stack.53.pos, bf16[1024,512]{1,0:T(8,128)(2,1)S(1)} %bitcast.41, f32[1024,512]{1,0:T(8,128)S(1)} %copy-done, bf16[512,512]{1,0:T(8,128)(2,1)S(1)} %copy-done.2, f32[1,512]{1,0:T(1,128)S(1)} %bitcast.47, f32[32,512]{1,0:T(8,128)S(1)} %copy-done.7, f32[32,512]{1,0:T(8,128)S(1)} %copy-done.9, ...), custom_call_target="tpu_custom_call" | custom-call | tf_op jit(solution)/shard_map/margins/pallas_call | solution.py:215
  22.6 38.6 %all-gather.1 = f32[8,2,1024]{2,1,0:T(2,128)S(1)} all-gather(f32[1,2,1024]{2,1,0:T(2,128)S(1)} %bitcast.46), channel_id=2, replica_groups=mesh['yl'=2,'c'=2,'yh'=2,'z'=8,'x'=4] {'yl','c','yh'}, dimensions={0}, use_global_device_ids=true | all-gather | bytes 73728 | tf_op jit(solution)/shard_map/all_gather | solution.py:224
  61.2 5.3 %sensitivities.1 = (bf16[2,4,160,1024]{3,2,1,0:T(8,128)(2,1)}, bf16[2,160,512]{2,1,0:T(8,128)(2,1)S(1)}, bf16[1024,512]{1,0:T(8,128)(2,1)S(1)}, bf16[512,512]{1,0:T(8,128)(2,1)S(1)}) custom-call(s32[6]{0:T(128)S(1)} %stack.53.pos, f32[4,2,2,1024]{3,2,1,0:T(2,128)S(1)} %bitcast.45, bf16[1024,512]{1,0:T(8,128)(2,1)S(1)} %bitcast.42, f32[1024,512]{1,0:T(8,128)S(1)} %copy-done, ...), custom_call_target="tpu_custom_call" | custom-call | tf_op jit(solution)/shard_map/sensitivities/pallas_call | solution.py:226
  66.5 0.2 collective-permute-start.5
  66.7 1.5 collective-permute-done.5
  68.2 0.1 add_convert_fusion
  68.3 0.1 pad_maximum_fusion
  68.3 35.4 %all_to_all.20 = bf16[4,320,512]{2,1,0:T(8,128)(2,1)} all-to-all(bf16[4,320,512]{2,1,0:T(8,128)(2,1)S(1)} %pad_maximum_fusion), channel_id=1, replica_groups=mesh['yl'=2,'c'=2,'yh'=2,'z'=8,'x'=4] {'x'}, dimensions={0} | all-to-all | bytes 2621440 | tf_op jit(solution)/shard_map/all_to_all | solution.py:173
  103.7 1.8 reduce_sum.21
  105.5 0.7 pad_maximum_fusion.1
  106.3 8.2 %all-to-all-start.1 = ((bf16[8,40,512]{2,1,0:T(8,128)(2,1)}), bf16[8,40,512]{2,1,0:T(8,128)(2,1)S(1)}, u32[]{:S(2)}, u32[]{:S(2)}) async-start(bf16[8,40,512]{2,1,0:T(8,128)(2,1)} %pad_maximum_fusion.1), calls=%async_computation.1 | async-start | bytes 655360 | tf_op jit(solution)/shard_map/all_to_all | solution.py:173
  114.5 12.7 %all-to-all-done.1 = bf16[8,40,512]{2,1,0:T(8,128)(2,1)S(1)} async-done(((bf16[8,40,512]{2,1,0:T(8,128)(2,1)}), bf16[8,40,512]{2,1,0:T(8,128)(2,1)S(1)}, u32[]{:S(2)}, u32[]{:S(2)}) %all-to-all-start.1) | async-done | bytes 327712 | tf_op jit(solution)/shard_map/all_to_all | solution.py:173
  127.3 2.9 %collective-permute-start.6 = (f32[20,512]{1,0:T(8,128)S(1)}, f32[20,512]{1,0:T(8,128)S(1)}, u32[]{:S(2)}, u32[]{:S(2)}) collective-permute-start(f32[20,512]{1,0:T(8,128)S(1)} %fusion.1), channel_id=1, source_target_pairs={{0,32},{32,0},{1,33},{33,1},{2,34},{34,2},{3,35},{35,3},{4,36},{36... | collective-permute-start | bytes 122888 | tf_op jit(solution)/shard_map/ppermute | solution.py:259
  130.2 2.9 %collective-permute-done.6 = f32[20,512]{1,0:T(8,128)S(1)} collective-permute-done((f32[20,512]{1,0:T(8,128)S(1)}, f32[20,512]{1,0:T(8,128)S(1)}, u32[]{:S(2)}, u32[]{:S(2)}) %collective-permute-start.6) | collective-permute-done | bytes 40992 | tf_op jit(solution)/shard_map/ppermute | solution.py:259
  133.1 0.8 collective-permute-start.7
  133.9 0.1 convert_element_type.42.v0
  134.0 1.4 collective-permute-start.2
  135.4 1.5 collective-permute-done.7
  137.0 3.1 %collective-permute-start.8 = (bf16[20,512]{1,0:T(8,128)(2,1)S(1)}, bf16[20,512]{1,0:T(8,128)(2,1)S(1)}, u32[]{:S(2)}, u32[]{:S(2)}) collective-permute-start(bf16[20,512]{1,0:T(8,128)(2,1)S(1)} %pad_maximum_fusion.2), channel_id=1, source_target_pairs={{0,32},{32,0},{1,33},{33,1},{2,34},{34,2},{3,35},{35,3},{4,36},{36... | collective-permute-start | bytes 61448 | tf_op jit(solution)/shard_map/ppermute | solution.py:262
  140.1 16.5 %collective-permute-done.8 = bf16[20,512]{1,0:T(8,128)(2,1)S(1)} collective-permute-done((bf16[20,512]{1,0:T(8,128)(2,1)S(1)}, bf16[20,512]{1,0:T(8,128)(2,1)S(1)}, u32[]{:S(2)}, u32[]{:S(2)}) %collective-permute-start.8) | collective-permute-done | bytes 20512 | tf_op jit(solution)/shard_map/ppermute | solution.py:262
  156.7 0.9 broadcast_in_dim.32
  157.6 3.6 %all-to-all-start.2 = ((bf16[8,2,20,512]{3,1,2,0:T(2,128)(2,1)}), bf16[8,2,20,512]{3,1,2,0:T(2,128)(2,1)S(1)}, u32[]{:S(2)}, u32[]{:S(2)}) async-start(bf16[8,2,20,512]{3,1,2,0:T(2,128)(2,1)} %broadcast_in_dim.32), calls=%async_computation.2 | async-start | bytes 655360 | tf_op jit(solution)/shard_map/all_to_all | solution.py:177
  161.2 0.0 collective-permute-start.1
  161.2 0.5 collective-permute-start.3
  161.7 10.7 %all-to-all-done.2 = bf16[8,2,20,512]{3,1,2,0:T(2,128)(2,1)S(1)} async-done(((bf16[8,2,20,512]{3,1,2,0:T(2,128)(2,1)}), bf16[8,2,20,512]{3,1,2,0:T(2,128)(2,1)S(1)}, u32[]{:S(2)}, u32[]{:S(2)}) %all-to-all-start.2) | async-done | bytes 327712 | tf_op jit(solution)/shard_map/all_to_all | solution.py:177
  172.4 0.1 copy.49
  172.5 0.0 copy-start.3
  172.5 1.2 broadcast_in_dim.33
  173.7 5.8 %all-to-all-start.3 = ((bf16[4,8,2,20,512]{4,1,3,2,0:T(8,128)(2,1)}), bf16[4,8,2,20,512]{4,1,3,2,0:T(8,128)(2,1)}, u32[]{:S(2)}, u32[]{:S(2)}) async-start(bf16[4,8,2,20,512]{4,1,3,2,0:T(8,128)(2,1)} %broadcast_in_dim.33), calls=%async_computation.3 | async-start | bytes 2621440 | tf_op jit(solution)/shard_map/all_to_all | solution.py:177
  179.5 0.0 all-gather.4.cloned.1.call-done
  179.5 16.1 %adjoints.1 = (f32[512,512]{1,0:T(8,128)S(1)}, bf16[512,512]{1,0:T(8,128)(2,1)S(1)}) custom-call(s32[6]{0:T(128)S(1)} %stack.53.pos, bf16[4,512,1024]{2,1,0:T(8,128)(2,1)} %bitcast.49, bf16[1024,512]{1,0:T(8,128)(2,1)S(1)} %convert_element_type.42.v0, bf16[1024,512]{1,0:T(8,128)(2,1)} %collective-permute-done.1.v1, ...), custom_call_target="tpu_custom_call" | custom-call | tf_op jit(solution)/shard_map/adjoints/pallas_call | solution.py:278
  195.6 0.0 copy-start.5
  195.6 1.0 copy-done.5
  196.6 1.9 collective-permute-start.4
  198.5 1.3 slice.43
  199.8 0.3 copy.53
  200.2 1.0 slice.44
  201.1 0.1 copy.51
  201.3 0.1 reshape.169
  201.4 0.3 collective-permute-start.9
  201.7 1.7 bitcast_convert_fusion
  203.4 1.1 convert_multiply_fusion
  204.5 2.8 %collective-permute-done.4 = bf16[512,512]{1,0:T(8,128)(2,1)S(1)} collective-permute-done((bf16[512,512]{1,0:T(8,128)(2,1)S(1)}, bf16[512,512]{1,0:T(8,128)(2,1)S(1)}, u32[]{:S(2)}, u32[]{:S(2)}) %collective-permute-start.4) | collective-permute-done | bytes 524320 | tf_op jit(solution)/shard_map/ppermute | solution.py:293
  207.3 0.1 bitcast_convert_fusion.1
  207.4 0.3 maximum_select_fusion
  207.7 3.5 %copy.52 = f32[1024,1,512]{2,1,0:T(1,128)} copy(f32[1024,1,512]{2,0,1:T(8,128)S(1)} %bitcast.48) | data formatting | bytes 4194304
  (36 shorter events, 0.2 us)
Async XLA Ops:
  7.2 172.3 %all-gather.4.cloned.1.call-start = ((), (), s32[]{:S(2)}) async-start(), calls=%async_computation.4 | async-start | bytes 4325376 | tf_op jit(solution)/shard_map/all_gather | solution.py:204
  7.2 1.6 collective-permute-start
  8.8 0.7 copy-start.11
  8.8 52.5 %copy-start.8 = (f32[32,512]{1,0:T(8,128)S(1)}, f32[32,512]{1,0:T(8,128)}, u32[]{:S(2)}) copy-start(f32[32,512]{1,0:T(8,128)} %load.3) | copy-start | bytes 196612
  8.8 52.5 %copy-start.10 = (f32[32,512]{1,0:T(8,128)S(1)}, f32[32,512]{1,0:T(8,128)}, u32[]{:S(2)}) copy-start(f32[32,512]{1,0:T(8,128)} %reset.3) | copy-start | bytes 196612
  14.0 1.6 copy-start
  15.6 1.0 copy-start.2
  16.6 1.2 copy-start.4
  17.9 0.8 copy-start.7
  18.7 0.8 copy-start.9
  66.5 1.6 collective-permute-start.5
  103.7 30.2 %copy-start.1 = (f32[1024,512]{1,0:T(8,128)S(1)}, f32[1024,512]{1,0:T(8,128)}, u32[]{:S(2)}) copy-start(f32[1024,512]{1,0:T(8,128)} %vol.3) | copy-start | bytes 6291460
  106.3 20.9 %all-to-all-start.1 = ((bf16[8,40,512]{2,1,0:T(8,128)(2,1)}), bf16[8,40,512]{2,1,0:T(8,128)(2,1)S(1)}, u32[]{:S(2)}, u32[]{:S(2)}) async-start(bf16[8,40,512]{2,1,0:T(8,128)(2,1)} %pad_maximum_fusion.1), calls=%async_computation.1 | async-start | bytes 655360 | tf_op jit(solution)/shard_map/all_to_all | solution.py:173
  127.3 5.8 %collective-permute-start.6 = (f32[20,512]{1,0:T(8,128)S(1)}, f32[20,512]{1,0:T(8,128)S(1)}, u32[]{:S(2)}, u32[]{:S(2)}) collective-permute-start(f32[20,512]{1,0:T(8,128)S(1)} %fusion.1), channel_id=1, source_target_pairs={{0,32},{32,0},{1,33},{33,1},{2,34},{34,2},{3,35},{35,3},{4,36},{36... | collective-permute-start | bytes 122888 | tf_op jit(solution)/shard_map/ppermute | solution.py:259
  133.1 3.9 %collective-permute-start.7 = (f32[4,512]{1,0:T(4,128)S(1)}, f32[4,512]{1,0:T(4,128)S(1)}, u32[]{:S(2)}, u32[]{:S(2)}) collective-permute-start(f32[4,512]{1,0:T(4,128)S(1)} %slice.42), channel_id=1, source_target_pairs={{0,128},{128,0},{1,129},{129,1},{2,130},{130,2},{3,131},{131,3},{4... | collective-permute-start | bytes 24584 | tf_op jit(solution)/shard_map/ppermute | solution.py:260
  134.0 27.2 %collective-permute-start.2 = (bf16[1024,512]{1,0:T(8,128)(2,1)S(1)}, bf16[1024,512]{1,0:T(8,128)(2,1)S(1)}, u32[]{:S(2)}, u32[]{:S(2)}) collective-permute-start(bf16[1024,512]{1,0:T(8,128)(2,1)S(1)} %convert_element_type.42.v0), channel_id=1, source_target_pairs={{0,128},{128,0},{1,129},{129,1},{2,130},{130,2},{3,131},{131,3},{4... | collective-permute-start | bytes 3145736 | tf_op jit(solution)/shard_map/ppermute | solution.py:207
  137.0 19.6 %collective-permute-start.8 = (bf16[20,512]{1,0:T(8,128)(2,1)S(1)}, bf16[20,512]{1,0:T(8,128)(2,1)S(1)}, u32[]{:S(2)}, u32[]{:S(2)}) collective-permute-start(bf16[20,512]{1,0:T(8,128)(2,1)S(1)} %pad_maximum_fusion.2), channel_id=1, source_target_pairs={{0,32},{32,0},{1,33},{33,1},{2,34},{34,2},{3,35},{35,3},{4,36},{36... | collective-permute-start | bytes 61448 | tf_op jit(solution)/shard_map/ppermute | solution.py:262
  157.6 14.8 %all-to-all-start.2 = ((bf16[8,2,20,512]{3,1,2,0:T(2,128)(2,1)}), bf16[8,2,20,512]{3,1,2,0:T(2,128)(2,1)S(1)}, u32[]{:S(2)}, u32[]{:S(2)}) async-start(bf16[8,2,20,512]{3,1,2,0:T(2,128)(2,1)} %broadcast_in_dim.32), calls=%async_computation.2 | async-start | bytes 655360 | tf_op jit(solution)/shard_map/all_to_all | solution.py:177
  161.2 18.3 %collective-permute-start.1 = (bf16[1024,512]{1,0:T(8,128)(2,1)S(1)}, bf16[1024,512]{1,0:T(8,128)(2,1)}, u32[]{:S(2)}, u32[]{:S(2)}) collective-permute-start(bf16[1024,512]{1,0:T(8,128)(2,1)S(1)} %convert_element_type.42.v0), channel_id=1, source_target_pairs={{0,64},{64,0},{1,65},{65,1},{2,66},{66,2},{3,67},{67,3},{4,68},{68... | collective-permute-start | bytes 3145736 | tf_op jit(solution)/shard_map/ppermute | solution.py:208
  161.2 18.3 %collective-permute-start.3 = (bf16[1024,512]{1,0:T(8,128)(2,1)S(1)}, bf16[1024,512]{1,0:T(8,128)(2,1)}, u32[]{:S(2)}, u32[]{:S(2)}) collective-permute-start(bf16[1024,512]{1,0:T(8,128)(2,1)S(1)} %collective-permute-done.2.v2), channel_id=1, source_target_pairs={{0,64},{64,0},{1,65},{65,1},{2,66},{66,2},{3,67},{67,3},{4,68},{68... | collective-permute-start | bytes 3145736 | tf_op jit(solution)/shard_map/ppermute | solution.py:209
  172.5 7.0 %copy-start.3 = (bf16[512,512]{1,0:T(8,128)(2,1)S(1)}, bf16[512,512]{1,0:T(8,128)(2,1)}, u32[]{:S(2)}) copy-start(bf16[512,512]{1,0:T(8,128)(2,1)} %chol.5) | copy-start | bytes 1572868
  173.7 24.8 %all-to-all-start.3 = ((bf16[4,8,2,20,512]{4,1,3,2,0:T(8,128)(2,1)}), bf16[4,8,2,20,512]{4,1,3,2,0:T(8,128)(2,1)}, u32[]{:S(2)}, u32[]{:S(2)}) async-start(bf16[4,8,2,20,512]{4,1,3,2,0:T(8,128)(2,1)} %broadcast_in_dim.33), calls=%async_computation.3 | async-start | bytes 2621440 | tf_op jit(solution)/shard_map/all_to_all | solution.py:177
  195.6 1.0 copy-start.5
  196.6 10.7 %collective-permute-start.4 = (bf16[512,512]{1,0:T(8,128)(2,1)S(1)}, bf16[512,512]{1,0:T(8,128)(2,1)S(1)}, u32[]{:S(2)}, u32[]{:S(2)}) collective-permute-start(bf16[512,512]{1,0:T(8,128)(2,1)S(1)} %get-tuple-element.12), channel_id=1, source_target_pairs={{0,32},{32,0},{1,33},{33,1},{2,34},{34,2},{3,35},{35,3},{4,36},{36... | collective-permute-start | bytes 1572872 | tf_op jit(solution)/shard_map/ppermute | solution.py:293
  201.4 2.0 collective-permute-start.9
  203.4 4.0 %copy-start.6 = (f32[512,512]{1,0:T(8,128)S(1)}, f32[512,512]{1,0:T(8,128)}, u32[]{:S(2)}) copy-start(f32[512,512]{1,0:T(8,128)} %copy-done.5) | copy-start | bytes 3145732
Sparse Core Ops, SparseCore 0:
  11.2 104.8 all-gather.3
